TPU v7x, 1024 devices: a whole 4x8x16 slice. The times are simulated.
1024 devices in a mesh: row: 16 (over x, y_lo), blk: 64 (over z, y_hi, core).
Axes of the slice: x: 4, y: 8 (y_hi: 2, y_lo: 4; y = y_hi * 4 + y_lo), z: 16, core: 2. Of those that a mesh axis runs over, the one named last changes fastest.
Arguments:
- state: float32 [16, 5, 16, 512, 128], P('row', None, None, 'blk'), may hold values from -6 to 6
- viscosity: float32 [16, 16, 512, 128], P('row', None, 'blk'), may hold values from 0.02 to 0.2
- coupling: float32 [16, 5, 5], P('row'), may hold values from -1.5 to 1.5
- offsets: int32 [4, 8], replicated, may hold values from 0 to 511
- live_span: int32 [16], P('row'), may hold values from 64 to 128, as said below
Outputs:
- updated: float32 [16, 5, 16, 512, 128], P('row', None, None, 'blk')
Inputs may be any that keep to these rules, and one draw needn't show every extreme that they name: `live_span`: every row has at least half of its 128 span cells fluid, and in every draw some row has all 128.
All inputs are finite; a program needn't handle non-finite values.
Results may differ from a plain program's by a relative error of at most 0.0001.
Values sent between devices are 32-bit elements; how exact they have to be, the bound alone decides.
A program may use at most 32 MiB of HBM per device.

v0:
```python
import math

import jax
import jax.numpy as jnp
from jax import lax
from jax.sharding import PartitionSpec as P

MODES = 5
SECTIONS = 4


section_alphas = (0.25, 1.0 / 3.0, 0.5, 1.0)
time_step = 0.25
speed_axial = 1.0
speed_pitch = 0.6
speed_span = 0.3


def extended(cells, sides, width):
    for axis, dim in sides:
        count = lax.axis_size(axis)
        head = lax.slice_in_dim(cells, 0, width, axis=dim)
        tail = lax.slice_in_dim(cells, cells.shape[dim] - width, cells.shape[dim], axis=dim)
        cells = jnp.concatenate(
            [
                lax.ppermute(tail, axis, [(i, (i + 1) % count) for i in range(count)]),
                cells,
                lax.ppermute(head, axis, [((i + 1) % count, i) for i in range(count)]),
            ],
            axis=dim,
        )
    return cells


def partner_2(value, axis, stride):
    mask = 2**stride
    pairs = [(source, source ^ mask) for source in range(lax.axis_size(axis))]
    return lax.ppermute(value, axis, pairs)


def basis_table(position, harmonics):
    rows = [jnp.ones_like(position)]
    for order in range(1, harmonics + 1):
        rows.append(jnp.cos(order * position))
    for order in range(1, harmonics + 1):
        rows.append(jnp.sin(order * position))
    return jnp.stack(rows)


def local_rates(field, ghost, viscosity, coupling, mask):
    padded = extended(field, (("blk", 3),), 1)
    up_axial = jnp.concatenate([field[:, :, 1:], ghost[:, :, None]], 2)
    down_axial = jnp.concatenate([field[:, :, :1], field[:, :, :-1]], 2)
    up_pitch = padded[:, :, :, 2:]
    down_pitch = padded[:, :, :, :-2]
    up_span = jnp.concatenate([field[..., 1:], field[..., -1:]], 4)
    down_span = jnp.concatenate([field[..., :1], field[..., :-1]], 4)
    advect = (
        speed_axial * (up_axial - field)
        - speed_pitch * (field - down_pitch)
        - speed_span * (field - down_span)
    )
    beside_all = up_axial + down_axial + up_pitch + down_pitch + up_span + down_span - 6.0 * field
    source = jnp.einsum("rvw,rwaps->rvaps", coupling, field, precision=lax.Precision.HIGHEST)
    return (advect + viscosity[:, None] * beside_all + source) * mask


def body(state, viscosity, coupling, offsets, live_span):
    blocks = lax.axis_size("blk")
    row_index = lax.axis_index("row")
    blk_index = lax.axis_index("blk")
    axial = state.shape[2]
    pitch = state.shape[3]
    span = state.shape[4]
    total_pitch = pitch * blocks
    cells = blk_index * pitch + jnp.arange(pitch)
    position = cells.astype(jnp.float32) * jnp.float32(2.0 * math.pi / total_pitch)
    basis = basis_table(position, MODES)
    weights = jnp.array([1.0 / total_pitch] + [2.0 / total_pitch] * (2 * MODES), jnp.float32)
    mask = (jnp.arange(span) < live_span[0]).astype(jnp.float32)[None, None, None, None, :]
    field = state
    for section in range(SECTIONS):
        strip = field[:, :, axial - 1]
        partner = partner_2(strip, "row", 0)
        turn = offsets[section, row_index // 2]
        offset = jnp.where(row_index % 2 == 0, turn, (total_pitch - turn) % total_pitch)
        circle = lax.all_gather(partner, "blk", axis=2, tiled=True)
        doubled = jnp.concatenate([circle, circle], 2)
        window = lax.dynamic_slice_in_dim(doubled, blk_index * pitch + offset, pitch, 2)
        partial_coef = (
            jnp.einsum("mi,rvis->rmvs", basis, window, precision=lax.Precision.HIGHEST)
            * weights[None, :, None, None]
        )
        coef = lax.psum(partial_coef, "blk")
        recon = jnp.einsum("mi,rmvs->rvis", basis, coef, precision=lax.Precision.HIGHEST)
        ghost = 0.5 * (window + recon)
        field = state + section_alphas[section] * time_step * local_rates(
            field, ghost, viscosity, coupling, mask
        )
    return field


def solution(mesh):
    in_specs = (
        P("row", None, None, "blk", None),
        P("row", None, "blk", None),
        P("row", None, None),
        P(),
        P("row"),
    )
    out_specs = P("row", None, None, "blk", None)
    return jax.shard_map(body, mesh=mesh, in_specs=in_specs, out_specs=out_specs, check_vma=False)
```

profile of v0, /device:TPU:1, one launch (start us, length us, event | category | flops | bytes accessed | tf_op | source)
XLA Modules:
  0.0 1952.7 jit_solution(17413765589231198669)
XLA Ops:
  6.5 0.8 slice_bitcast_fusion.3
  7.3 4.0 collective-permute-start
  11.4 1.2 collective-permute-done
  12.5 0.6 copy-done.9
  13.2 1.1 fusion.137
  14.4 9.3 collective-permute-start.1
  23.7 9.1 collective-permute-start.2
  32.9 1.5 constant_dynamic-slice_fusion.1
  35.1 1.0 copy.34
  37.8 1.4 fusion.26
  39.6 130.3 %all-gather.5.cloned.1.call-done = f32[1,5,512,128]{3,2,1,0:T(8,128)} async-done(((f32[1,5,8,128]{3,2,1,0:T(8,128)}), f32[1,5,512,128]{3,2,1,0:T(8,128)}) %all-gather.5.cloned.1.call-update) | async-done | bytes 1310736 | tf_op jit(solution)/shard_map/all_gather | solution.py:87
  169.9 0.8 fusion.91
  170.9 325.0 %psum.28 = f32[11,5,128]{2,0,1:T(8,128)S(1)} all-reduce(f32[11,5,128]{2,0,1:T(8,128)S(1)} %fusion.7), channel_id=1, replica_groups=mesh['row'=16,'blk'=64] {'blk'}, use_global_device_ids=true, to_apply=%region_0.1 | all-reduce | flops 7040 | bytes 56320 | tf_op jit(solution)/shard_map/psum | solution.py:94
  496.2 0.6 copy-done.7
  496.8 1.3 fusion.83
  498.1 3.6 collective-permute-start.3
  501.6 1.5 collective-permute-done.3
  503.1 0.6 copy-done.11
  505.2 8.1 collective-permute-start.4
  513.3 4.7 collective-permute-start.5
  518.7 0.6 fusion.24
  519.3 133.8 %all-gather.7.cloned.1.call-done = f32[1,5,512,128]{3,2,1,0:T(8,128)} async-done(((f32[1,5,8,128]{3,2,1,0:T(8,128)}), f32[1,5,512,128]{3,2,1,0:T(8,128)}) %all-gather.7.cloned.1.call-update) | async-done | bytes 1310736 | tf_op jit(solution)/shard_map/all_gather | solution.py:87
  653.1 0.8 fusion.90
  654.2 325.0 %psum.29 = f32[11,5,128]{2,0,1:T(8,128)S(1)} all-reduce(f32[11,5,128]{2,0,1:T(8,128)S(1)} %fusion.5), channel_id=1, replica_groups=mesh['row'=16,'blk'=64] {'blk'}, use_global_device_ids=true, to_apply=%region_1.2 | all-reduce | flops 7040 | bytes 56320 | tf_op jit(solution)/shard_map/psum | solution.py:94
  979.4 0.6 copy-done.3
  980.0 1.3 fusion.68
  981.3 3.6 collective-permute-start.6
  984.8 1.5 collective-permute-done.6
  986.3 0.6 copy-done.12
  988.2 8.1 collective-permute-start.7
  996.3 4.7 collective-permute-start.8
  1001.3 0.6 fusion.22
  1001.9 134.0 %all-gather.9.cloned.1.call-done = f32[1,5,512,128]{3,2,1,0:T(8,128)} async-done(((f32[1,5,8,128]{3,2,1,0:T(8,128)}), f32[1,5,512,128]{3,2,1,0:T(8,128)}) %all-gather.9.cloned.1.call-update) | async-done | bytes 1310736 | tf_op jit(solution)/shard_map/all_gather | solution.py:87
  1135.9 0.8 fusion.89
  1136.9 325.4 %psum.30 = f32[11,5,128]{2,0,1:T(8,128)S(1)} all-reduce(f32[11,5,128]{2,0,1:T(8,128)S(1)} %fusion.3), channel_id=1, replica_groups=mesh['row'=16,'blk'=64] {'blk'}, use_global_device_ids=true, to_apply=%region_2.3 | all-reduce | flops 7040 | bytes 56320 | tf_op jit(solution)/shard_map/psum | solution.py:94
  1462.5 0.6 copy-done.4
  1463.1 1.3 fusion.53
  1464.4 3.2 collective-permute-start.9
  1467.6 1.6 collective-permute-done.9
  1469.2 0.6 copy-done.10
  1471.2 8.1 collective-permute-start.10
  1479.3 4.7 collective-permute-start.11
  1484.3 0.6 fusion.20
  1484.9 133.7 %all-gather.11.cloned.1.call-done = f32[1,5,512,128]{3,2,1,0:T(8,128)} async-done(((f32[1,5,8,128]{3,2,1,0:T(8,128)}), f32[1,5,512,128]{3,2,1,0:T(8,128)}) %all-gather.11.cloned.1.call-update) | async-done | bytes 1310736 | tf_op jit(solution)/shard_map/all_gather | solution.py:87
  1618.7 0.8 fusion.88
  1619.7 325.0 %psum.31 = f32[11,5,128]{2,0,1:T(8,128)S(1)} all-reduce(f32[11,5,128]{2,0,1:T(8,128)S(1)} %fusion.1), channel_id=1, replica_groups=mesh['row'=16,'blk'=64] {'blk'}, use_global_device_ids=true, to_apply=%region_3.4 | all-reduce | flops 7040 | bytes 56320 | tf_op jit(solution)/shard_map/psum | solution.py:94
  1944.9 0.5 fusion.38
  1945.4 0.7 copy.35
  (71 shorter events, 4.2 us)
Async XLA Ops:
  6.5 31.2 %copy-start = (f32[1,5,16,8,128]{4,3,2,1,0:T(8,128)S(1)}, f32[1,5,16,8,128]{4,3,2,1,0:T(8,128)}, u32[]{:S(2)}) copy-start(f32[1,5,16,8,128]{4,3,2,1,0:T(8,128)} %param.6) | copy-start | bytes 983044
  6.5 163.3 %all-gather.5.cloned.1.call-start = ((), (), s32[]{:S(2)}) async-start(), calls=%async_computation | async-start | bytes 1331200 | tf_op jit(solution)/shard_map/all_gather | solution.py:87
  7.3 5.2 collective-permute-start
  12.5 0.6 copy-start.9
  13.2 640.0 %all-gather.7.cloned.1.call-start = ((), (), s32[]{:S(2)}) async-start(), calls=%async_computation.1 | async-start | bytes 1331200 | tf_op jit(solution)/shard_map/all_gather | solution.py:87
  14.4 481.8 %collective-permute-start.1 = (f32[1,5,16,1,128]{4,3,1,2,0:T(1,128)S(1)}, f32[1,5,16,1,128]{4,3,1,2,0:T(1,128)S(1)}, u32[]{:S(2)}, u32[]{:S(2)}) collective-permute-start(f32[1,5,16,1,128]{4,3,1,2,0:T(1,128)S(1)} %get-tuple-element.43), channel_id=1, source_target_pairs={{0,1},{1,2},{2,3},{3,4},{4,5},{5,6},{6,7},{7,8},{8,9},{9,10},{10,1... | collective-permute-start | bytes 122888 | tf_op jit(solution)/shard_map/ppermute | solution.py:26
  23.7 472.5 %collective-permute-start.2 = (f32[1,5,16,1,128]{4,3,1,2,0:T(1,128)S(1)}, f32[1,5,16,1,128]{4,3,1,2,0:T(1,128)S(1)}, u32[]{:S(2)}, u32[]{:S(2)}) collective-permute-start(f32[1,5,16,1,128]{4,3,1,2,0:T(1,128)S(1)} %get-tuple-element.44), channel_id=1, source_target_pairs={{1,0},{2,1},{3,2},{4,3},{5,4},{6,5},{7,6},{8,7},{9,8},{10,9},{11,1... | collective-permute-start | bytes 122888 | tf_op jit(solution)/shard_map/ppermute | solution.py:28
  39.4 131.3 %copy-start.13 = (f32[11]{0:T(128)S(1)}, f32[11]{0:T(128)}, u32[]{:S(2)}) copy-start(f32[11]{0:T(128)} %constant.109.clone) | copy-start | bytes 136
  39.4 457.4 %copy-start.1 = (f32[1,16,8,128]{3,2,1,0:T(8,128)S(1)}, f32[1,16,8,128]{3,2,1,0:T(8,128)}, u32[]{:S(2)}) copy-start(f32[1,16,8,128]{3,2,1,0:T(8,128)} %param.7) | copy-start | bytes 196612
  496.1 0.6 copy-start.7
  496.2 0.6 copy-start.8
  498.1 5.0 collective-permute-start.3
  503.1 0.6 copy-start.11
  503.7 632.2 %all-gather.9.cloned.1.call-start = ((), (), s32[]{:S(2)}) async-start(), calls=%async_computation.2 | async-start | bytes 1331200 | tf_op jit(solution)/shard_map/all_gather | solution.py:87
  505.2 474.2 %collective-permute-start.4 = (f32[1,5,16,1,128]{4,3,1,2,0:T(1,128)S(1)}, f32[1,5,16,1,128]{4,3,1,2,0:T(1,128)S(1)}, u32[]{:S(2)}, u32[]{:S(2)}) collective-permute-start(f32[1,5,16,1,128]{4,3,1,2,0:T(1,128)S(1)} %get-tuple-element.33), channel_id=1, source_target_pairs={{0,1},{1,2},{2,3},{3,4},{4,5},{5,6},{6,7},{7,8},{8,9},{9,10},{10,1... | collective-permute-start | bytes 122888 | tf_op jit(solution)/shard_map/ppermute | solution.py:26
  513.3 466.1 %collective-permute-start.5 = (f32[1,5,16,1,128]{4,3,1,2,0:T(1,128)S(1)}, f32[1,5,16,1,128]{4,3,1,2,0:T(1,128)S(1)}, u32[]{:S(2)}, u32[]{:S(2)}) collective-permute-start(f32[1,5,16,1,128]{4,3,1,2,0:T(1,128)S(1)} %get-tuple-element.34), channel_id=1, source_target_pairs={{1,0},{2,1},{3,2},{4,3},{5,4},{6,5},{7,6},{8,7},{9,8},{10,9},{11,1... | collective-permute-start | bytes 122888 | tf_op jit(solution)/shard_map/ppermute | solution.py:28
  518.0 0.7 copy-start.2
  979.4 0.6 copy-start.3
  979.4 0.6 copy-start.5
  981.3 5.0 collective-permute-start.6
  986.3 0.6 copy-start.12
  986.9 631.7 %all-gather.11.cloned.1.call-start = ((), (), s32[]{:S(2)}) async-start(), calls=%async_computation.3 | async-start | bytes 1331200 | tf_op jit(solution)/shard_map/all_gather | solution.py:87
  988.2 474.3 %collective-permute-start.7 = (f32[1,5,16,1,128]{4,3,1,2,0:T(1,128)S(1)}, f32[1,5,16,1,128]{4,3,1,2,0:T(1,128)S(1)}, u32[]{:S(2)}, u32[]{:S(2)}) collective-permute-start(f32[1,5,16,1,128]{4,3,1,2,0:T(1,128)S(1)} %get-tuple-element.23), channel_id=1, source_target_pairs={{0,1},{1,2},{2,3},{3,4},{4,5},{5,6},{6,7},{7,8},{8,9},{9,10},{10,1... | collective-permute-start | bytes 122888 | tf_op jit(solution)/shard_map/ppermute | solution.py:26
  996.3 466.2 %collective-permute-start.8 = (f32[1,5,16,1,128]{4,3,1,2,0:T(1,128)S(1)}, f32[1,5,16,1,128]{4,3,1,2,0:T(1,128)S(1)}, u32[]{:S(2)}, u32[]{:S(2)}) collective-permute-start(f32[1,5,16,1,128]{4,3,1,2,0:T(1,128)S(1)} %get-tuple-element.24), channel_id=1, source_target_pairs={{1,0},{2,1},{3,2},{4,3},{5,4},{6,5},{7,6},{8,7},{9,8},{10,9},{11,1... | collective-permute-start | bytes 122888 | tf_op jit(solution)/shard_map/ppermute | solution.py:28
  1462.5 0.6 copy-start.4
  1462.5 0.6 copy-start.6
  1464.4 4.8 collective-permute-start.9
  1469.2 0.6 copy-start.10
  1471.2 473.8 %collective-permute-start.10 = (f32[1,5,16,1,128]{4,3,1,2,0:T(1,128)S(1)}, f32[1,5,16,1,128]{4,3,1,2,0:T(1,128)S(1)}, u32[]{:S(2)}, u32[]{:S(2)}) collective-permute-start(f32[1,5,16,1,128]{4,3,1,2,0:T(1,128)S(1)} %get-tuple-element.13), channel_id=1, source_target_pairs={{0,1},{1,2},{2,3},{3,4},{4,5},{5,6},{6,7},{7,8},{8,9},{9,10},{10,1... | collective-permute-start | bytes 122888 | tf_op jit(solution)/shard_map/ppermute | solution.py:26
  1479.3 465.7 %collective-permute-start.11 = (f32[1,5,16,1,128]{4,3,1,2,0:T(1,128)S(1)}, f32[1,5,16,1,128]{4,3,1,2,0:T(1,128)S(1)}, u32[]{:S(2)}, u32[]{:S(2)}) collective-permute-start(f32[1,5,16,1,128]{4,3,1,2,0:T(1,128)S(1)} %get-tuple-element.14), channel_id=1, source_target_pairs={{1,0},{2,1},{3,2},{4,3},{5,4},{6,5},{7,6},{8,7},{9,8},{10,9},{11,1... | collective-permute-start | bytes 122888 | tf_op jit(solution)/shard_map/ppermute | solution.py:28
Sparse Core Ops, SparseCore 0:
  13.3 156.5 all-gather.4
  503.8 149.2 all-gather.6
  987.1 148.7 all-gather.8
  1470.0 148.6 all-gather.10
where the time goes:
time: 1960 us; the launch traced here: 1950 us
  blocking collectives  1300 us (66%)
  waiting for transfers between devices  538 us (27%)
  starting transfers between devices  71.2 us (4%)
    psum x4, blocking collectives, body(): coef = lax.psum(partial_coef, 'blk')  1300 us
    all_gather x4, waiting for transfers between devices, body(): circle = lax.all_gather(partner, 'blk', axis=2, tiled=True)  532 us
  transfers between devices with their start and end apart: 16, of which 8 were waited for; matrix products, arithmetic and copies ran while one was open for 1% of the time, Pallas kernels for 0%

commit v1 on v0

v1 whole, which is shorter than its diff:
```python
import functools
import math

import jax
import jax.numpy as jnp
import numpy as np
from jax import lax
from jax.experimental import pallas as pl
from jax.experimental.pallas import tpu as pltpu
from jax.sharding import PartitionSpec as P

MESH = pl.DeviceIdType.MESH
MODES = 5
SECTIONS = 4
NVAR = 5
AXIAL = 16
PITCH = 8
SPAN = 128
BLOCKS = 64
NP = BLOCKS * PITCH
SLICES = 16
CHUNK = 64
PAD = 8

section_alphas = (0.25, 1.0 / 3.0, 0.5, 1.0)
time_step = 0.25
speed_axial = 1.0
speed_pitch = 0.6
speed_span = 0.3
HIGHEST = lax.Precision.HIGHEST


def basis_tables():
    theta = np.arange(NP) * (2.0 * math.pi / NP)
    rows = [np.ones(NP)]
    rows += [np.cos(j * theta) for j in range(1, MODES + 1)]
    rows += [np.sin(j * theta) for j in range(1, MODES + 1)]
    table = np.zeros((16, NP))
    table[: 2 * MODES + 1] = np.stack(rows)
    weights = np.full((16, 1), 2.0 / NP)
    weights[0] = 1.0 / NP
    return (table * weights).astype(np.float32), table.T.astype(np.float32).copy()


def worker_of(pair, s):
    return 2 * pair + (s // 2) % 2, 4 * s + 2 * (s % 2)


def kernel(
    state, visc, coup, offs, live, basis, basis_t, out,
    msg, recv, cst, hs, hr, vb, xa, xb, xc, hb, st, gbuf, fld, vext, gx,
    main_s, main_r, cst_s, cst_r, halo_s, halo_r, ret_s, ret_r,
):
    row = lax.axis_index("row")
    blk = lax.axis_index("blk")
    pair, parity = row // 2, row % 2
    z = blk // 4
    own_row, own_blk = worker_of(pair, z)
    is_worker = jnp.logical_and(own_row == row, own_blk == blk)
    after, before = (blk + 1) % BLOCKS, (blk + BLOCKS - 1) % BLOCKS

    bar = pltpu.get_barrier_semaphore()

    def greet(r, b):
        pl.semaphore_signal(bar, inc=1, device_id=(r, b), device_id_type=MESH)

    @pl.when(is_worker)
    def _():
        def greet_source(i, c):
            at = (blk + BLOCKS // 2 + i) % BLOCKS
            greet(row ^ 1, at)

            @pl.when(at != blk)
            def _():
                greet(row, at)

            return c

        lax.fori_loop(0, BLOCKS, greet_source, 0)

    for i in range(SLICES):
        s = (z + SLICES // 2 + i) % SLICES
        wr, wb = worker_of(pair, s)

        @pl.when(jnp.logical_not(jnp.logical_and(wr == row, wb == blk)))
        def _():
            greet(wr, wb)

    greet(row, after)
    greet(row, before)
    greet(row ^ 1, blk)

    lane8 = lax.broadcasted_iota(jnp.int32, (8, 128), 1)
    slot8 = lane8 // 16
    top = AXIAL - 1
    tiles = (
        [(v, top) for v in range(NVAR)] + [(-1, top), (-1, top - 1), (-1, top - 2)],
        [(v, top - 1) for v in range(NVAR)] + [(0, top - 3), (1, top - 3), (2, top - 3)],
        [(v, top - 2) for v in range(NVAR)] + [(3, top - 3), (4, top - 3)],
    )
    for t, slots in enumerate(tiles):
        values = [visc[a] if v < 0 else state[v, a] for v, a in slots]
        for s in range(SLICES):
            packed = jnp.zeros((8, 128), jnp.float32)
            for q, value in enumerate(values):
                turn = (16 * q - (8 * s - 4)) % 128
                moved = pltpu.roll(value, turn, 1) if turn else value
                packed = jnp.where(slot8 == q, moved, packed)
            msg[s, t] = packed

    sub8 = lax.broadcasted_iota(jnp.int32, (8, 128), 0)
    table = jnp.zeros((8, 128), jnp.float32)
    for v in range(NVAR):
        for w in range(NVAR):
            here = jnp.logical_and(slot8 == v, sub8 == (w - v) % 8)
            table = jnp.where(here, coup[v, w], table)
    cst[parity, 0:8] = table
    cst[parity, 8:16] = jnp.full((8, 128), live[0].astype(jnp.float32))

    def pack_halo(j, c):
        for v in range(NVAR + 1):
            for h in range(2):
                if v < NVAR:
                    low = state[v, 2 * j + h, 0:4]
                    high = state[v, 2 * j + h, 4:8]
                else:
                    low = visc[2 * j + h, 0:4]
                    high = visc[2 * j + h, 4:8]
                hs[0, v, j, 4 * h : 4 * h + 4] = high
                hs[1, v, j, 4 * h : 4 * h + 4] = low
        return c

    lax.fori_loop(0, AXIAL // 2, pack_halo, 0)

    pl.semaphore_wait(bar, SLICES + 3 + jnp.where(is_worker, 2 * BLOCKS - 2, 0))

    mine = pl.ds(pl.multiple_of(PAD + PITCH * blk, 8), PITCH)

    def send_main(i, c):
        s = (z + SLICES // 2 + jnp.where(i % 2 == 1, (i + 1) // 2, SLICES - i // 2)) % SLICES
        wr, wb = worker_of(pair, s)
        self = jnp.logical_and(wr == row, wb == blk)

        @pl.when(jnp.logical_not(self))
        def _():
            pltpu.make_async_remote_copy(
                src_ref=msg.at[s],
                dst_ref=recv.at[parity, :, mine],
                send_sem=main_s,
                recv_sem=main_r,
                device_id=(wr, wb),
                device_id_type=MESH,
            ).start()

        return c

    lax.fori_loop(0, SLICES, send_main, 0)

    def const_copy():
        return pltpu.make_async_remote_copy(
            src_ref=cst.at[parity],
            dst_ref=cst.at[parity],
            send_sem=cst_s,
            recv_sem=cst_r,
            device_id=(row ^ 1, blk),
            device_id_type=MESH,
        )

    const_copy().start()

    def wait_bytes(ref, sem):
        pltpu.make_async_copy(ref, ref, sem).wait()

    @pl.when(is_worker)
    def _():
        wait_bytes(msg.at[pl.ds(0, SLICES - 1)], main_s)

    @pl.when(jnp.logical_not(is_worker))
    def _():
        wait_bytes(msg, main_s)

    def halo_copy(side):
        return pltpu.make_async_remote_copy(
            src_ref=hs.at[side],
            dst_ref=hr.at[side],
            send_sem=halo_s.at[side],
            recv_sem=halo_r.at[side],
            device_id=(row, after if side == 0 else before),
            device_id_type=MESH,
        )

    halo_copy(0).start()
    halo_copy(1).start()
    const_copy().wait_send()
    wait_bytes(cst.at[1 - parity], cst_r)

    @pl.when(is_worker)
    def _():
        recv[parity, :, mine] = msg[z]
        wait_bytes(st.at[pl.ds(0, 2 * BLOCKS - 1)], main_r)
        lane = lax.broadcasted_iota(jnp.int32, (CHUNK, 128), 1)
        slot = lane // 16
        cell = 8 * z - 4 + lane % 16
        first, last = cell == 0, cell == SPAN - 1
        cell_f = cell[0:1].astype(jnp.float32)

        def wrap(ref, *index):
            ref[(*index, slice(PAD - 1, PAD))] = ref[(*index, slice(PAD + NP - 1, PAD + NP))]
            ref[(*index, slice(PAD + NP, PAD + NP + 1))] = ref[(*index, slice(PAD, PAD + 1))]

        shifts = []
        for k in range(SECTIONS):
            turn = offs[k, pair]
            shifts.append((turn, (NP - turn) % NP))

        def widen(value, q):
            value = jnp.where(slot == q, value, 0.0)
            for step in (16, 32, 64):
                value = value + pltpu.roll(value, step, 1)
            return value

        for rho in range(2):
            for t in range(3):
                wrap(recv, rho, t)

            def spread(i, c):
                at = pl.multiple_of(i * CHUNK, CHUNK)
                packed = recv[rho, 0, pl.ds(PAD + at, CHUNK)]
                for q in range(3):
                    vb[rho, q, pl.ds(at, CHUNK)] = widen(packed, 5 + q)
                return c

            lax.fori_loop(0, NP // CHUNK, spread, 0)

        fields = [
            [[(recv, (rho, t)) for t in range(3)] for rho in range(2)],
            [[(xa, (rho, t)) for t in range(3)] for rho in range(2)],
            [[(xb, (rho, t)) for t in range(2)] for rho in range(2)],
            [[(xc, (rho,))] for rho in range(2)],
        ]
        for k in range(SECTIONS):
            for rho in range(2):
                ref, index = fields[k][rho][0]
                strip = ref[(*index, slice(PAD, PAD + NP))]
                coef = jnp.dot(basis[...], strip, precision=HIGHEST, preferred_element_type=jnp.float32)
                recon = jnp.dot(basis_t[...], coef, precision=HIGHEST, preferred_element_type=jnp.float32)
                half = 0.5 * (strip + recon)
                hb[k, rho, 0:NP] = half
                hb[k, rho, NP : NP + CHUNK] = half[0:CHUNK]
            if k == SECTIONS - 1:
                break
            factor = section_alphas[k] * time_step
            for rho in range(2):
                table = cst[rho]
                scale = jnp.where(cell_f < table[8:9], factor, 0.0)

                def update(i, c):
                    at = pl.multiple_of(i * CHUNK, CHUNK)

                    def take(t, move=0):
                        ref, index = fields[k][rho][t]
                        return ref[(*index, pl.ds(PAD + at + move, CHUNK))]

                    inner = [take(t) for t in range(3 - k)]
                    start = (at + shifts[k][rho]) % NP
                    ghost = hb[k, 1 - rho, pl.ds(start, CHUNK)]
                    for t in range(3 - k):
                        here = inner[t]
                        up_axial = ghost if t == 0 else inner[t - 1]
                        if t + 1 < 3 - k:
                            down_axial = inner[t + 1]
                        elif k == 0:
                            two = recv[rho, 1, pl.ds(PAD + at, CHUNK)]
                            three = recv[rho, 2, pl.ds(PAD + at, CHUNK)]
                            down_axial = jnp.where(
                                slot < 3, pltpu.roll(two, 48, 1), pltpu.roll(three, 96, 1)
                            )
                        else:
                            down_axial = take(t + 1)
                        up_pitch, down_pitch = take(t, 1), take(t, -1)
                        up_span = jnp.where(last, here, pltpu.roll(here, 127, 1))
                        down_span = jnp.where(first, here, pltpu.roll(here, 1, 1))
                        rate = (
                            speed_axial * (up_axial - here)
                            - speed_pitch * (here - down_pitch)
                            - speed_span * (here - down_span)
                        )
                        beside = up_axial + down_axial + up_pitch + down_pitch + up_span + down_span
                        rate = rate + vb[rho, t, pl.ds(at, CHUNK)] * (beside - 6.0 * here)
                        rate = rate + table[0:1] * here
                        for d in range(1, 8):
                            rate = rate + table[d : d + 1] * pltpu.roll(here, 128 - 16 * d, 1)
                        ref, index = fields[k + 1][rho][t] if t < 3 - k else None
                        ref[(*index, pl.ds(PAD + at, CHUNK))] = (
                            recv[rho, t, pl.ds(PAD + at, CHUNK)] + scale * rate
                        )
                    return c

                lax.fori_loop(0, NP // CHUNK, update, 0)
                for t in range(3 - k):
                    ref, index = fields[k + 1][rho][t]
                    wrap(ref, *index)

        lane16 = lax.broadcasted_iota(jnp.int32, (16, 128), 1)
        inside = jnp.logical_and(lane16 % 16 >= 4, lane16 % 16 < 12)

        def send_back(i, c):
            at = (blk + BLOCKS // 2 + jnp.where(i % 2 == 1, (i + 1) // 2, BLOCKS - i // 2)) % BLOCKS
            for rho in range(2):
                part = []
                for k in range(SECTIONS):
                    back = 4 if k < 3 else 0
                    start = (PITCH * at + NP - back + shifts[k][rho]) % NP
                    part.append(hb[k, 1 - rho, pl.ds(start, 16 if k < 3 else 8)])
                both = jnp.where(inside, part[0], pltpu.roll(part[1], 8, 1))
                third = jnp.where(inside, pltpu.roll(part[2], 80, 1), pltpu.roll(part[2], 40, 1))
                both = jnp.where(lane16 < 84, both, third)
                to = rho * BLOCKS + at
                st[to, 0] = both[0:8]
                st[to, 1] = both[8:16]
                st[to, 2] = part[3]
                other = rho * 1 + pair * 2
                self = jnp.logical_and(other == row, at == blk)

                @pl.when(jnp.logical_not(self))
                def _():
                    pltpu.make_async_remote_copy(
                        src_ref=st.at[to],
                        dst_ref=gbuf.at[z],
                        send_sem=ret_s,
                        recv_sem=ret_r,
                        device_id=(other, at),
                        device_id_type=MESH,
                    ).start()

            return c

        lax.fori_loop(0, BLOCKS, send_back, 0)
        gbuf[z] = st[parity * BLOCKS + blk]

    halo_copy(0).wait_recv()
    halo_copy(1).wait_recv()

    def widen_block(j, c):
        for h in range(2):
            a = 2 * j + h
            part = slice(4 * h, 4 * h + 4)
            for v in range(NVAR):
                fld[0, v, a, 0:4] = hr[0, v, j, part]
                fld[0, v, a, 4:12] = state[v, a]
                fld[0, v, a, 12:16] = hr[1, v, j, part]
            vext[a, 0:4] = hr[0, NVAR, j, part]
            vext[a, 4:12] = visc[a]
            vext[a, 12:16] = hr[1, NVAR, j, part]
        return c

    lax.fori_loop(0, AXIAL // 2, widen_block, 0)

    lane2 = lax.broadcasted_iota(jnp.int32, (16, 128), 1)
    first2, last2 = lane2 == 0, lane2 == SPAN - 1
    alive = lane2 < live[0]
    cs = [[coup[v, w] for w in range(NVAR)] for v in range(NVAR)]

    def layer(k, a, up):
        here = [fld[k, v, a] for v in range(NVAR)]
        vis = vext[a]
        below = jnp.maximum(a - 1, 0)
        scale = jnp.where(alive, section_alphas[k] * time_step, 0.0)
        for v in range(NVAR):
            u = here[v]
            up_axial, down_axial = up(v), fld[k, v, below]
            up_pitch, down_pitch = pltpu.roll(u, 15, 0), pltpu.roll(u, 1, 0)
            up_span = jnp.where(last2, u, pltpu.roll(u, 127, 1))
            down_span = jnp.where(first2, u, pltpu.roll(u, 1, 1))
            rate = (
                speed_axial * (up_axial - u)
                - speed_pitch * (u - down_pitch)
                - speed_span * (u - down_span)
            )
            beside = up_axial + down_axial + up_pitch + down_pitch + up_span + down_span
            rate = rate + vis * (beside - 6.0 * u)
            for w in range(NVAR):
                rate = rate + cs[v][w] * here[w]
            new = fld[0, v, a] + scale * rate
            if k < SECTIONS - 1:
                fld[k + 1, v, a] = new
            else:
                out[v, a] = pltpu.roll(new, 12, 0)[0:8]

    for k in range(SECTIONS):

        def inner_layer(a, c):
            layer(k, a, lambda v: fld[k, v, a + 1])
            return c

        lax.fori_loop(0, AXIAL - 1 - k, inner_layer, 0)

    @pl.when(is_worker)
    def _():
        wait_bytes(gbuf.at[pl.ds(0, SLICES - 1)], ret_r)

    @pl.when(jnp.logical_not(is_worker))
    def _():
        wait_bytes(gbuf, ret_r)

    group8 = lane8 // 8
    for v in range(NVAR):
        places = [16 * v + 4, 16 * v + 12]
        places.append(84 + 16 * v if v < 3 else 92 + 16 * (v - 3))
        for k in range(3):
            for half in range(2):
                value = jnp.zeros((8, 128), jnp.float32)
                for s in range(SLICES):
                    turn = (8 * s - places[k]) % 128
                    value = jnp.where(group8 == s, pltpu.roll(gbuf[s, half], turn, 1), value)
                gx[k, v, 8 * half : 8 * half + 8] = value
        value = jnp.zeros((8, 128), jnp.float32)
        for s in range(SLICES):
            turn = (8 * s - (16 * v + 4)) % 128
            value = jnp.where(group8 == s, pltpu.roll(gbuf[s, 2], turn, 1), value)
        gx[3, v, 0:4] = jnp.zeros((4, 128), jnp.float32)
        gx[3, v, 4:12] = value
        gx[3, v, 12:16] = jnp.zeros((4, 128), jnp.float32)

    for k in range(SECTIONS):
        for a in range(AXIAL - 1 - k, AXIAL - 1):
            layer(k, a, lambda v: fld[k, v, a + 1])
        layer(k, AXIAL - 1, lambda v: gx[k, v])

    halo_copy(0).wait_send()
    halo_copy(1).wait_send()

    @pl.when(is_worker)
    def _():
        wait_bytes(st.at[pl.ds(0, 2 * BLOCKS - 1)], ret_s)


def solution(mesh):
    weighted, plain = basis_tables()

    def body(state, visc, coup, offs, live):
        vmem = pl.BlockSpec(memory_space=pltpu.VMEM)
        smem = pl.BlockSpec(memory_space=pltpu.SMEM)
        f32 = jnp.float32
        done = pl.pallas_call(
            kernel,
            out_shape=jax.ShapeDtypeStruct((NVAR, AXIAL, PITCH, SPAN), f32),
            in_specs=[vmem, vmem, smem, smem, smem, vmem, vmem],
            out_specs=vmem,
            scratch_shapes=[
                pltpu.VMEM((SLICES, 3, 8, 128), f32),
                pltpu.VMEM((2, 3, NP + 2 * PAD, 128), f32),
                pltpu.VMEM((2, 16, 128), f32),
                pltpu.VMEM((2, NVAR + 1, AXIAL // 2, 8, 128), f32),
                pltpu.VMEM((2, NVAR + 1, AXIAL // 2, 8, 128), f32),
                pltpu.VMEM((2, 3, NP, 128), f32),
                pltpu.VMEM((2, 3, NP + 2 * PAD, 128), f32),
                pltpu.VMEM((2, 2, NP + 2 * PAD, 128), f32),
                pltpu.VMEM((2, NP + 2 * PAD, 128), f32),
                pltpu.VMEM((SECTIONS, 2, NP + CHUNK, 128), f32),
                pltpu.VMEM((2 * BLOCKS, 3, 8, 128), f32),
                pltpu.VMEM((SLICES, 3, 8, 128), f32),
                pltpu.VMEM((SECTIONS, NVAR, AXIAL, 16, 128), f32),
                pltpu.VMEM((AXIAL, 16, 128), f32),
                pltpu.VMEM((SECTIONS, NVAR, 16, 128), f32),
                pltpu.SemaphoreType.DMA,
                pltpu.SemaphoreType.DMA,
                pltpu.SemaphoreType.DMA,
                pltpu.SemaphoreType.DMA,
                pltpu.SemaphoreType.DMA((2,)),
                pltpu.SemaphoreType.DMA((2,)),
                pltpu.SemaphoreType.DMA,
                pltpu.SemaphoreType.DMA,
            ],
            compiler_params=pltpu.CompilerParams(
                collective_id=0, has_side_effects=True, vmem_limit_bytes=48 << 20
            ),
            name="sections",
        )(state[0], visc[0], coup[0], offs, live, jnp.asarray(weighted), jnp.asarray(plain))
        return done[None]

    in_specs = (
        P("row", None, None, "blk", None),
        P("row", None, "blk", None),
        P("row", None, None),
        P(),
        P("row"),
    )
    out_specs = P("row", None, None, "blk", None)
    return jax.shard_map(body, mesh=mesh, in_specs=in_specs, out_specs=out_specs, check_vma=False)
```

time: 1960 us -> 95.5 us (0.05)
  the two profiles are of different devices: /device:TPU:1 before, /device:TPU:16 now
where the time goes in v1:
time: 95.5 us; the launch traced here: 95.1 us
  Pallas kernels  89.5 us (94%)
  local copies, waits for them, and re-layouts  4.93 us (5%)
    pallas_call x1, Pallas kernels, body(): pl.pallas_call(kernel, out_shape=jax.ShapeDtypeStruct((NVAR, AXIAL, PITCH...  89.5 us
    unnamed x14, local copies, waits for them, and re-layouts  4.93 us

profile of v1, /device:TPU:16, one launch (start us, length us, event | category | flops | bytes accessed | tf_op | source)
XLA Modules:
  0.0 95.1 jit_solution(17057093400874830554)
XLA Ops:
  0.0 0.0 copy-start.5
  0.7 0.0 copy-done.5
  0.7 0.0 copy-start.4
  0.7 0.7 copy-done.4
  1.4 0.0 copy-start
  1.4 1.0 %copy-done = f32[1,5,16,8,128]{4,3,2,1,0:T(8,128)S(1)} copy-done((f32[1,5,16,8,128]{4,3,2,1,0:T(8,128)S(1)}, f32[1,5,16,8,128]{4,3,2,1,0:T(8,128)}, u32[]{:S(2)}) %copy-start) | copy-done | bytes 327704
  2.3 0.0 copy-start.1
  2.3 0.9 copy-done.1
  3.3 0.0 copy-start.2
  3.3 0.8 copy-done.2
  4.1 0.0 copy-start.3
  4.1 0.8 copy-done.3
  4.9 89.5 %sections.1 = f32[5,16,8,128]{3,2,1,0:T(8,128)S(1)} custom-call(f32[5,16,8,128]{3,2,1,0:T(8,128)S(1)} %bitcast.7, f32[16,8,128]{2,1,0:T(8,128)S(1)} %bitcast.8, f32[5,5]{1,0:T(8,128)S(1)} %bitcast.9, s32[4,8]{1,0:T(4,128)S(1)} %copy-done.4, s32[1]{0:T(128)S(6)} %copy.12.live, f32[16,512]{1,0:T(8,128)S(1)} %copy-done.3, f32[512,16]{1,0:T(8,128)S(1)} %copy-done.1), custom_call_target="tpu_custom_call" | custom-call | tf_op jit(solution)/shard_map/sections/pallas_call | solution.py:445
  94.4 0.7 copy.13
  (1 shorter events, 0.0 us)
Async XLA Ops:
  0.0 0.7 copy-start.5
  0.7 0.7 copy-start.4
  1.4 1.0 %copy-start = (f32[1,5,16,8,128]{4,3,2,1,0:T(8,128)S(1)}, f32[1,5,16,8,128]{4,3,2,1,0:T(8,128)}, u32[]{:S(2)}) copy-start(f32[1,5,16,8,128]{4,3,2,1,0:T(8,128)} %param.7) | copy-start | bytes 983044
  2.3 0.9 copy-start.1
  3.3 0.8 copy-start.2
  4.1 0.8 copy-start.3

commit v2 on v1

--- a/solution.py
+++ b/solution.py
@@ -19,7 +19,8 @@
 BLOCKS = 64
 NP = BLOCKS * PITCH
 SLICES = 16
-CHUNK = 64
+CHUNK = 128
+WRAP = 128
 PAD = 8
 
 section_alphas = (0.25, 1.0 / 3.0, 0.5, 1.0)
@@ -27,7 +28,10 @@
 speed_axial = 1.0
 speed_pitch = 0.6
 speed_span = 0.3
-HIGHEST = lax.Precision.HIGHEST
+
+def split(value):
+    high = value.astype(jnp.bfloat16)
+    return high, (value - high.astype(jnp.float32)).astype(jnp.bfloat16)
 
 
 def basis_tables():
@@ -35,11 +39,19 @@
     rows = [np.ones(NP)]
     rows += [np.cos(j * theta) for j in range(1, MODES + 1)]
     rows += [np.sin(j * theta) for j in range(1, MODES + 1)]
-    table = np.zeros((16, NP))
+    table = np.zeros((16, NP), np.float32)
     table[: 2 * MODES + 1] = np.stack(rows)
-    weights = np.full((16, 1), 2.0 / NP)
+    weights = np.full((16, 1), 2.0 / NP, np.float32)
     weights[0] = 1.0 / NP
-    return (table * weights).astype(np.float32), table.T.astype(np.float32).copy()
+
+    def parts(value):
+        high = value.astype(jnp.bfloat16)
+        return high, (value - high.astype(np.float32)).astype(jnp.bfloat16)
+
+    back = np.zeros((NP, 128), jnp.bfloat16)
+    high, low = parts(np.ascontiguousarray(table.T))
+    back[:, 0:16], back[:, 16:32], back[:, 32:48] = high, low, high
+    return np.concatenate(parts(table * weights)), back
 
 
 def worker_of(pair, s):
@@ -47,10 +59,19 @@
 
 
 def kernel(
-    state, visc, coup, offs, live, basis, basis_t, out,
+    state_hbm, visc_hbm, coup, offs, live, basis_hbm, basis_t_hbm, out,
+    state, visc, basis, basis_t, mix, load_s,
     msg, recv, cst, hs, hr, vb, xa, xb, xc, hb, st, gbuf, fld, vext, gx,
     main_s, main_r, cst_s, cst_r, halo_s, halo_r, ret_s, ret_r,
 ):
+    loads = [
+        pltpu.make_async_copy(source, target, load_s.at[i])
+        for i, (source, target) in enumerate(
+            [(state_hbm, state), (visc_hbm, visc), (basis_hbm, basis), (basis_t_hbm, basis_t)]
+        )
+    ]
+    for load in loads:
+        load.start()
     row = lax.axis_index("row")
     blk = lax.axis_index("blk")
     pair, parity = row // 2, row % 2
@@ -89,6 +110,9 @@
     greet(row, after)
     greet(row, before)
     greet(row ^ 1, blk)
+
+    for load in loads:
+        load.wait()
 
     lane8 = lax.broadcasted_iota(jnp.int32, (8, 128), 1)
     slot8 = lane8 // 16
@@ -113,7 +137,7 @@
     for v in range(NVAR):
         for w in range(NVAR):
             here = jnp.logical_and(slot8 == v, sub8 == (w - v) % 8)
-            table = jnp.where(here, coup[v, w], table)
+            table = jnp.where(here, coup[v, 0, w], table)
     cst[parity, 0:8] = table
     cst[parity, 8:16] = jnp.full((8, 128), live[0].astype(jnp.float32))
 
@@ -197,11 +221,34 @@
     @pl.when(is_worker)
     def _():
         recv[parity, :, mine] = msg[z]
+        source = lax.broadcasted_iota(jnp.int32, (128, 128), 0)
+        target = lax.broadcasted_iota(jnp.int32, (128, 128), 1)
+        place = 8 * z - 4 + target % 16
+        lower = jnp.where(place == 0, target, target - 1)
+        upper = jnp.where(place == SPAN - 1, target, target + 1)
+
+        def one(here):
+            return jnp.where(here, 1.0, 0.0)
+
+        around = one(source == lower) + one(source == upper) - 6.0 * one(source == target)
+        still = speed_span * one(source == lower) - (
+            speed_axial + speed_pitch + speed_span
+        ) * one(source == target)
+        for rho in range(2):
+            both = still
+            for d in range(8):
+                both = both + jnp.where(
+                    source == (target + 16 * d) % 128, cst[rho, d : d + 1], 0.0
+                )
+            high, low = split(both)
+            for half in range(2):
+                mix[rho, 128 * half : 128 * half + 128, 0:128] = high
+                mix[rho, 128 * half : 128 * half + 128, 128:256] = around.astype(jnp.bfloat16)
+            mix[rho, 256:384, 0:128] = low
         wait_bytes(st.at[pl.ds(0, 2 * BLOCKS - 1)], main_r)
         lane = lax.broadcasted_iota(jnp.int32, (CHUNK, 128), 1)
         slot = lane // 16
         cell = 8 * z - 4 + lane % 16
-        first, last = cell == 0, cell == SPAN - 1
         cell_f = cell[0:1].astype(jnp.float32)
 
         def wrap(ref, *index):
@@ -239,14 +286,22 @@
             [[(xc, (rho,))] for rho in range(2)],
         ]
         for k in range(SECTIONS):
+            strips = []
             for rho in range(2):
                 ref, index = fields[k][rho][0]
-                strip = ref[(*index, slice(PAD, PAD + NP))]
-                coef = jnp.dot(basis[...], strip, precision=HIGHEST, preferred_element_type=jnp.float32)
-                recon = jnp.dot(basis_t[...], coef, precision=HIGHEST, preferred_element_type=jnp.float32)
-                half = 0.5 * (strip + recon)
-                hb[k, rho, 0:NP] = half
-                hb[k, rho, NP : NP + CHUNK] = half[0:CHUNK]
+                strips.append(ref[(*index, slice(PAD, PAD + NP))])
+            strips = jnp.concatenate(strips, 1)
+            high, low = split(strips)
+            sums = jnp.dot(basis[...], high, preferred_element_type=jnp.float32)
+            coef = sums[0:16] + sums[16:32]
+            coef = coef + jnp.dot(basis[0:16], low, preferred_element_type=jnp.float32)
+            high, low = split(coef)
+            coefs = jnp.concatenate([high, high, low, jnp.zeros((80, 256), jnp.bfloat16)], 0)
+            recon = jnp.dot(basis_t[...], coefs, preferred_element_type=jnp.float32)
+            half = 0.5 * (strips + recon)
+            for rho in range(2):
+                hb[k, rho, 0:NP] = half[:, 128 * rho : 128 * rho + 128]
+                hb[k, rho, NP : NP + WRAP] = half[0:WRAP, 128 * rho : 128 * rho + 128]
             if k == SECTIONS - 1:
                 break
             factor = section_alphas[k] * time_step
@@ -278,19 +333,17 @@
                         else:
                             down_axial = take(t + 1)
                         up_pitch, down_pitch = take(t, 1), take(t, -1)
-                        up_span = jnp.where(last, here, pltpu.roll(here, 127, 1))
-                        down_span = jnp.where(first, here, pltpu.roll(here, 1, 1))
-                        rate = (
-                            speed_axial * (up_axial - here)
-                            - speed_pitch * (here - down_pitch)
-                            - speed_span * (here - down_span)
+                        high, low = split(here)
+                        linear = jnp.dot(
+                            jnp.concatenate([high, low], 1),
+                            mix[rho, 0:256],
+                            preferred_element_type=jnp.float32,
                         )
-                        beside = up_axial + down_axial + up_pitch + down_pitch + up_span + down_span
-                        rate = rate + vb[rho, t, pl.ds(at, CHUNK)] * (beside - 6.0 * here)
-                        rate = rate + table[0:1] * here
-                        for d in range(1, 8):
-                            rate = rate + table[d : d + 1] * pltpu.roll(here, 128 - 16 * d, 1)
-                        ref, index = fields[k + 1][rho][t] if t < 3 - k else None
+                        low = jnp.dot(high, mix[rho, 256:384, 0:128], preferred_element_type=jnp.float32)
+                        beside = up_axial + down_axial + up_pitch + down_pitch + linear[:, 128:256]
+                        rate = speed_axial * up_axial + speed_pitch * down_pitch + low
+                        rate = rate + linear[:, 0:128] + vb[rho, t, pl.ds(at, CHUNK)] * beside
+                        ref, index = fields[k + 1][rho][t]
                         ref[(*index, pl.ds(PAD + at, CHUNK))] = (
                             recv[rho, t, pl.ds(PAD + at, CHUNK)] + scale * rate
                         )
@@ -359,7 +412,7 @@
     lane2 = lax.broadcasted_iota(jnp.int32, (16, 128), 1)
     first2, last2 = lane2 == 0, lane2 == SPAN - 1
     alive = lane2 < live[0]
-    cs = [[coup[v, w] for w in range(NVAR)] for v in range(NVAR)]
+    cs = [[coup[v, 0, w] for w in range(NVAR)] for v in range(NVAR)]
 
     def layer(k, a, up):
         here = [fld[k, v, a] for v in range(NVAR)]
@@ -440,14 +493,21 @@
 
     def body(state, visc, coup, offs, live):
         vmem = pl.BlockSpec(memory_space=pltpu.VMEM)
+        hbm = pl.BlockSpec(memory_space=pltpu.HBM)
         smem = pl.BlockSpec(memory_space=pltpu.SMEM)
         f32 = jnp.float32
         done = pl.pallas_call(
             kernel,
             out_shape=jax.ShapeDtypeStruct((NVAR, AXIAL, PITCH, SPAN), f32),
-            in_specs=[vmem, vmem, smem, smem, smem, vmem, vmem],
+            in_specs=[hbm, hbm, smem, smem, smem, hbm, hbm],
             out_specs=vmem,
             scratch_shapes=[
+                pltpu.VMEM((NVAR, AXIAL, PITCH, SPAN), f32),
+                pltpu.VMEM((AXIAL, PITCH, SPAN), f32),
+                pltpu.VMEM((32, NP), jnp.bfloat16),
+                pltpu.VMEM((NP, 128), jnp.bfloat16),
+                pltpu.VMEM((2, 384, 256), jnp.bfloat16),
+                pltpu.SemaphoreType.DMA((4,)),
                 pltpu.VMEM((SLICES, 3, 8, 128), f32),
                 pltpu.VMEM((2, 3, NP + 2 * PAD, 128), f32),
                 pltpu.VMEM((2, 16, 128), f32),
@@ -457,7 +517,7 @@
                 pltpu.VMEM((2, 3, NP + 2 * PAD, 128), f32),
                 pltpu.VMEM((2, 2, NP + 2 * PAD, 128), f32),
                 pltpu.VMEM((2, NP + 2 * PAD, 128), f32),
-                pltpu.VMEM((SECTIONS, 2, NP + CHUNK, 128), f32),
+                pltpu.VMEM((SECTIONS, 2, NP + WRAP, 128), f32),
                 pltpu.VMEM((2 * BLOCKS, 3, 8, 128), f32),
                 pltpu.VMEM((SLICES, 3, 8, 128), f32),
                 pltpu.VMEM((SECTIONS, NVAR, AXIAL, 16, 128), f32),
@@ -473,10 +533,10 @@
                 pltpu.SemaphoreType.DMA,
             ],
             compiler_params=pltpu.CompilerParams(
-                collective_id=0, has_side_effects=True, vmem_limit_bytes=48 << 20
+                collective_id=0, has_side_effects=True, vmem_limit_bytes=63 << 20
             ),
             name="sections",
-        )(state[0], visc[0], coup[0], offs, live, jnp.asarray(weighted), jnp.asarray(plain))
+        )(state[0], visc[0], jnp.transpose(coup, (1, 0, 2)), offs, live, jnp.asarray(weighted), jnp.asarray(plain))
         return done[None]
 
     in_specs = (

time: 95.5 us -> 84 us (0.88)
  Pallas kernels: 89.5 us -> 81.4 us
  local copies, waits for them, and re-layouts: 4.93 us -> 1.72 us
    pallas_call x1, Pallas kernels: 89.5 us -> 81.4 us  [body(): pl.pallas_call(kernel, out_shape=jax.ShapeDtypeStruct((NVAR, AXIAL, PITCH...]
    unnamed x14 -> x1, local copies, waits for them, and re-layouts: 4.93 us -> 1.72 us
where the time goes in v2:
time: 84 us; the launch traced here: 83.8 us
  Pallas kernels  81.4 us (97%)
  local copies, waits for them, and re-layouts  1.72 us (2%)
    pallas_call x1, Pallas kernels, body(): pl.pallas_call(kernel, out_shape=jax.ShapeDtypeStruct((NVAR, AXIAL, PITCH...  81.4 us
    unnamed x1, local copies, waits for them, and re-layouts  1.72 us

profile of v2, /device:TPU:16, one launch (start us, length us, event | category | flops | bytes accessed | tf_op | source)
XLA Modules:
  0.0 83.8 jit_solution(15533797440156946561)
XLA Ops:
  0.7 81.4 %sections.1 = f32[5,16,8,128]{3,2,1,0:T(8,128)} custom-call(f32[5,16,8,128]{3,2,1,0:T(8,128)} %bitcast.5, f32[16,8,128]{2,1,0:T(8,128)} %bitcast.6, f32[5,1,5]{2,1,0:T(1,128)} %bitcast.7, s32[4,8]{1,0:T(4,128)} %offs.1, s32[1]{0:T(128)S(6)} %copy.9.live, bf16[32,512]{1,0:T(8,128)(2,1)} %constant.4.clone.basis_hbm, bf16[512,128]{1,0:T(8,128)(2,1)} %constant.5.clone.basis_t_hbm), custom_call_target="tpu_custom_call" | custom-call | tf_op jit(solution)/shard_map/sections/pallas_call | solution.py:499
  82.1 1.7 %copy.10 = f32[1,5,16,8,128]{4,3,2,1,0:T(8,128)} copy(f32[1,5,16,8,128]{4,3,2,1,0:T(8,128)} %bitcast.4) | data formatting | bytes 655360

commit v3 on v2

--- a/solution.py
+++ b/solution.py
@@ -19,8 +19,8 @@
 BLOCKS = 64
 NP = BLOCKS * PITCH
 SLICES = 16
-CHUNK = 128
-WRAP = 128
+CHUNK = 512
+WRAP = 512
 PAD = 8
 
 section_alphas = (0.25, 1.0 / 3.0, 0.5, 1.0)
@@ -60,7 +60,7 @@
 
 def kernel(
     state_hbm, visc_hbm, coup, offs, live, basis_hbm, basis_t_hbm, out,
-    state, visc, basis, basis_t, mix, load_s,
+    state, visc, basis, basis_t, mix, size, load_s,
     msg, recv, cst, hs, hr, vb, xa, xb, xc, hb, st, gbuf, fld, vext, gx,
     main_s, main_r, cst_s, cst_r, halo_s, halo_r, ret_s, ret_r,
 ):
@@ -80,6 +80,8 @@
     is_worker = jnp.logical_and(own_row == row, own_blk == blk)
     after, before = (blk + 1) % BLOCKS, (blk + BLOCKS - 1) % BLOCKS
 
+    many = size.at[pl.ds(0, 2 * BLOCKS - 1)]
+
     bar = pltpu.get_barrier_semaphore()
 
     def greet(r, b):
@@ -88,7 +90,7 @@
     @pl.when(is_worker)
     def _():
         def greet_source(i, c):
-            at = (blk + BLOCKS // 2 + i) % BLOCKS
+            at = (blk + BLOCKS // 2 + jnp.where(i % 2 == 1, (i + 1) // 2, BLOCKS - i // 2)) % BLOCKS
             greet(row ^ 1, at)
 
             @pl.when(at != blk)
@@ -244,8 +246,11 @@
             for half in range(2):
                 mix[rho, 128 * half : 128 * half + 128, 0:128] = high
                 mix[rho, 128 * half : 128 * half + 128, 128:256] = around.astype(jnp.bfloat16)
+                for q in range(3):
+                    wide = one(source == 16 * (5 + q) + target % 16).astype(jnp.bfloat16)
+                    mix[rho, 128 * half : 128 * half + 128, 256 + 128 * q : 384 + 128 * q] = wide
             mix[rho, 256:384, 0:128] = low
-        wait_bytes(st.at[pl.ds(0, 2 * BLOCKS - 1)], main_r)
+        wait_bytes(many, main_r)
         lane = lax.broadcasted_iota(jnp.int32, (CHUNK, 128), 1)
         slot = lane // 16
         cell = 8 * z - 4 + lane % 16
@@ -260,24 +265,9 @@
             turn = offs[k, pair]
             shifts.append((turn, (NP - turn) % NP))
 
-        def widen(value, q):
-            value = jnp.where(slot == q, value, 0.0)
-            for step in (16, 32, 64):
-                value = value + pltpu.roll(value, step, 1)
-            return value
-
         for rho in range(2):
             for t in range(3):
                 wrap(recv, rho, t)
-
-            def spread(i, c):
-                at = pl.multiple_of(i * CHUNK, CHUNK)
-                packed = recv[rho, 0, pl.ds(PAD + at, CHUNK)]
-                for q in range(3):
-                    vb[rho, q, pl.ds(at, CHUNK)] = widen(packed, 5 + q)
-                return c
-
-            lax.fori_loop(0, NP // CHUNK, spread, 0)
 
         fields = [
             [[(recv, (rho, t)) for t in range(3)] for rho in range(2)],
@@ -317,6 +307,7 @@
                         return ref[(*index, pl.ds(PAD + at + move, CHUNK))]
 
                     inner = [take(t) for t in range(3 - k)]
+                    vis = [vb[rho, t, pl.ds(at, CHUNK)] for t in range(3 - k)] if k else None
                     start = (at + shifts[k][rho]) % NP
                     ghost = hb[k, 1 - rho, pl.ds(start, CHUNK)]
                     for t in range(3 - k):
@@ -334,15 +325,20 @@
                             down_axial = take(t + 1)
                         up_pitch, down_pitch = take(t, 1), take(t, -1)
                         high, low = split(here)
+                        first = k == 0 and t == 0
                         linear = jnp.dot(
                             jnp.concatenate([high, low], 1),
-                            mix[rho, 0:256],
+                            mix[rho, 0:256] if first else mix[rho, 0:256, 0:256],
                             preferred_element_type=jnp.float32,
                         )
+                        if first:
+                            vis = [linear[:, 256 + 128 * q : 384 + 128 * q] for q in range(3)]
+                            for q in range(2):
+                                vb[rho, q, pl.ds(at, CHUNK)] = vis[q]
                         low = jnp.dot(high, mix[rho, 256:384, 0:128], preferred_element_type=jnp.float32)
                         beside = up_axial + down_axial + up_pitch + down_pitch + linear[:, 128:256]
                         rate = speed_axial * up_axial + speed_pitch * down_pitch + low
-                        rate = rate + linear[:, 0:128] + vb[rho, t, pl.ds(at, CHUNK)] * beside
+                        rate = rate + linear[:, 0:128] + vis[t] * beside
                         ref, index = fields[k + 1][rho][t]
                         ref[(*index, pl.ds(PAD + at, CHUNK))] = (
                             recv[rho, t, pl.ds(PAD + at, CHUNK)] + scale * rate
@@ -354,31 +350,38 @@
                     ref, index = fields[k + 1][rho][t]
                     wrap(ref, *index)
 
-        lane16 = lax.broadcasted_iota(jnp.int32, (16, 128), 1)
-        inside = jnp.logical_and(lane16 % 16 >= 4, lane16 % 16 < 12)
-
-        def send_back(i, c):
-            at = (blk + BLOCKS // 2 + jnp.where(i % 2 == 1, (i + 1) // 2, BLOCKS - i // 2)) % BLOCKS
-            for rho in range(2):
+        inside = jnp.logical_and(lane % 16 >= 4, lane % 16 < 12)
+        for rho in range(2):
+
+            def pack_back(i, c):
+                at = pl.multiple_of(i * CHUNK, CHUNK)
                 part = []
                 for k in range(SECTIONS):
                     back = 4 if k < 3 else 0
-                    start = (PITCH * at + NP - back + shifts[k][rho]) % NP
-                    part.append(hb[k, 1 - rho, pl.ds(start, 16 if k < 3 else 8)])
+                    start = (at + NP - back + shifts[k][rho]) % NP
+                    part.append(hb[k, 1 - rho, pl.ds(start, CHUNK)])
                 both = jnp.where(inside, part[0], pltpu.roll(part[1], 8, 1))
                 third = jnp.where(inside, pltpu.roll(part[2], 80, 1), pltpu.roll(part[2], 40, 1))
-                both = jnp.where(lane16 < 84, both, third)
-                to = rho * BLOCKS + at
-                st[to, 0] = both[0:8]
-                st[to, 1] = both[8:16]
-                st[to, 2] = part[3]
-                other = rho * 1 + pair * 2
-                self = jnp.logical_and(other == row, at == blk)
-
-                @pl.when(jnp.logical_not(self))
+                both = jnp.where(lane < 84, both, third)
+                st[rho, 0, pl.ds(at, CHUNK)] = both
+                st[rho, 1, pl.ds(at, CHUNK - 8)] = both[8:CHUNK]
+                before_at = pl.multiple_of((at + NP - 8) % NP, 8)
+                st[rho, 1, pl.ds(before_at, 8)] = both[0:8]
+                st[rho, 2, pl.ds(at, CHUNK)] = part[3]
+                return c
+
+            lax.fori_loop(0, NP // CHUNK, pack_back, 0)
+
+        def send_back(i, c):
+            at = (blk + BLOCKS // 2 + jnp.where(i % 2 == 1, (i + 1) // 2, BLOCKS - i // 2)) % BLOCKS
+            source_rows = pl.ds(pl.multiple_of(PITCH * at, 8), PITCH)
+            for rho in range(2):
+                other = 2 * pair + rho
+
+                @pl.when(jnp.logical_not(jnp.logical_and(other == row, at == blk)))
                 def _():
                     pltpu.make_async_remote_copy(
-                        src_ref=st.at[to],
+                        src_ref=st.at[rho, :, source_rows],
                         dst_ref=gbuf.at[z],
                         send_sem=ret_s,
                         recv_sem=ret_r,
@@ -389,7 +392,7 @@
             return c
 
         lax.fori_loop(0, BLOCKS, send_back, 0)
-        gbuf[z] = st[parity * BLOCKS + blk]
+        gbuf[z] = st[parity, :, pl.ds(pl.multiple_of(PITCH * blk, 8), PITCH)]
 
     halo_copy(0).wait_recv()
     halo_copy(1).wait_recv()
@@ -485,7 +488,7 @@
 
     @pl.when(is_worker)
     def _():
-        wait_bytes(st.at[pl.ds(0, 2 * BLOCKS - 1)], ret_s)
+        wait_bytes(many, ret_s)
 
 
 def solution(mesh):
@@ -506,19 +509,20 @@
                 pltpu.VMEM((AXIAL, PITCH, SPAN), f32),
                 pltpu.VMEM((32, NP), jnp.bfloat16),
                 pltpu.VMEM((NP, 128), jnp.bfloat16),
-                pltpu.VMEM((2, 384, 256), jnp.bfloat16),
+                pltpu.VMEM((2, 384, 640), jnp.bfloat16),
+                pltpu.VMEM((2 * BLOCKS, 3, 8, 128), f32),
                 pltpu.SemaphoreType.DMA((4,)),
                 pltpu.VMEM((SLICES, 3, 8, 128), f32),
                 pltpu.VMEM((2, 3, NP + 2 * PAD, 128), f32),
                 pltpu.VMEM((2, 16, 128), f32),
                 pltpu.VMEM((2, NVAR + 1, AXIAL // 2, 8, 128), f32),
                 pltpu.VMEM((2, NVAR + 1, AXIAL // 2, 8, 128), f32),
-                pltpu.VMEM((2, 3, NP, 128), f32),
+                pltpu.VMEM((2, 2, NP, 128), f32),
                 pltpu.VMEM((2, 3, NP + 2 * PAD, 128), f32),
                 pltpu.VMEM((2, 2, NP + 2 * PAD, 128), f32),
                 pltpu.VMEM((2, NP + 2 * PAD, 128), f32),
                 pltpu.VMEM((SECTIONS, 2, NP + WRAP, 128), f32),
-                pltpu.VMEM((2 * BLOCKS, 3, 8, 128), f32),
+                pltpu.VMEM((2, 3, NP, 128), f32),
                 pltpu.VMEM((SLICES, 3, 8, 128), f32),
                 pltpu.VMEM((SECTIONS, NVAR, AXIAL, 16, 128), f32),
                 pltpu.VMEM((AXIAL, 16, 128), f32),

time: 84 us -> 75.1 us (0.89)
  the two profiles are of different devices: /device:TPU:16 before, /device:TPU:1 now
where the time goes in v3:
time: 75.1 us; the launch traced here: 74.9 us
  Pallas kernels  72.5 us (97%)
  local copies, waits for them, and re-layouts  1.72 us (2%)
    pallas_call x1, Pallas kernels, body(): pl.pallas_call(kernel, out_shape=jax.ShapeDtypeStruct((NVAR, AXIAL, PITCH...  72.5 us
    unnamed x1, local copies, waits for them, and re-layouts  1.72 us

profile of v3, /device:TPU:1, one launch (start us, length us, event | category | flops | bytes accessed | tf_op | source)
XLA Modules:
  0.0 74.9 jit_solution(8852886790320353485)
XLA Ops:
  0.7 72.5 %sections.1 = f32[5,16,8,128]{3,2,1,0:T(8,128)} custom-call(f32[5,16,8,128]{3,2,1,0:T(8,128)} %bitcast.5, f32[16,8,128]{2,1,0:T(8,128)} %bitcast.6, f32[5,1,5]{2,1,0:T(1,128)} %bitcast.7, s32[4,8]{1,0:T(4,128)} %offs.1, s32[1]{0:T(128)S(6)} %copy.9.live, bf16[32,512]{1,0:T(8,128)(2,1)} %constant.4.clone.basis_hbm, bf16[512,128]{1,0:T(8,128)(2,1)} %constant.5.clone.basis_t_hbm), custom_call_target="tpu_custom_call" | custom-call | tf_op jit(solution)/shard_map/sections/pallas_call | solution.py:502
  73.2 1.7 %copy.10 = f32[1,5,16,8,128]{4,3,2,1,0:T(8,128)} copy(f32[1,5,16,8,128]{4,3,2,1,0:T(8,128)} %bitcast.4) | data formatting | bytes 655360

commit v4 on v3

--- a/solution.py
+++ b/solution.py
@@ -55,14 +55,14 @@
 
 
 def worker_of(pair, s):
-    return 2 * pair + (s // 2) % 2, 4 * s + 2 * (s % 2)
+    return 2 * pair + (s // 2) % 2, 4 * s + 2 * (s % 2) + 1
 
 
 def kernel(
     state_hbm, visc_hbm, coup, offs, live, basis_hbm, basis_t_hbm, out,
     state, visc, basis, basis_t, mix, size, load_s,
-    msg, recv, cst, hs, hr, vb, xa, xb, xc, hb, st, gbuf, fld, vext, gx,
-    main_s, main_r, cst_s, cst_r, halo_s, halo_r, ret_s, ret_r,
+    msg, recv, hs, hr, vb, xa, xb, xc, hb, st, gbuf, fld, vext, gx,
+    main_s, main_r, ready, halo_s, halo_r, ret_s, ret_r,
 ):
     loads = [
         pltpu.make_async_copy(source, target, load_s.at[i])
@@ -101,17 +101,7 @@
 
         lax.fori_loop(0, BLOCKS, greet_source, 0)
 
-    for i in range(SLICES):
-        s = (z + SLICES // 2 + i) % SLICES
-        wr, wb = worker_of(pair, s)
-
-        @pl.when(jnp.logical_not(jnp.logical_and(wr == row, wb == blk)))
-        def _():
-            greet(wr, wb)
-
     greet(row, after)
-    greet(row, before)
-    greet(row ^ 1, blk)
 
     for load in loads:
         load.wait()
@@ -124,24 +114,21 @@
         [(v, top - 1) for v in range(NVAR)] + [(0, top - 3), (1, top - 3), (2, top - 3)],
         [(v, top - 2) for v in range(NVAR)] + [(3, top - 3), (4, top - 3)],
     )
+    sub8 = lax.broadcasted_iota(jnp.int32, (8, 128), 0)
+    consts = jnp.where(lane8 == 112 + NVAR, live[0].astype(jnp.float32), 0.0)
+    for v in range(NVAR):
+        for w in range(NVAR):
+            here = jnp.logical_and(lane8 == 112 + v, sub8 == (w - v) % 8)
+            consts = jnp.where(here, coup[v, 0, w], consts)
     for t, slots in enumerate(tiles):
         values = [visc[a] if v < 0 else state[v, a] for v, a in slots]
         for s in range(SLICES):
-            packed = jnp.zeros((8, 128), jnp.float32)
+            packed = consts if t == 2 else jnp.zeros((8, 128), jnp.float32)
             for q, value in enumerate(values):
                 turn = (16 * q - (8 * s - 4)) % 128
                 moved = pltpu.roll(value, turn, 1) if turn else value
                 packed = jnp.where(slot8 == q, moved, packed)
             msg[s, t] = packed
-
-    sub8 = lax.broadcasted_iota(jnp.int32, (8, 128), 0)
-    table = jnp.zeros((8, 128), jnp.float32)
-    for v in range(NVAR):
-        for w in range(NVAR):
-            here = jnp.logical_and(slot8 == v, sub8 == (w - v) % 8)
-            table = jnp.where(here, coup[v, 0, w], table)
-    cst[parity, 0:8] = table
-    cst[parity, 8:16] = jnp.full((8, 128), live[0].astype(jnp.float32))
 
     def pack_halo(j, c):
         for v in range(NVAR + 1):
@@ -158,7 +145,8 @@
 
     lax.fori_loop(0, AXIAL // 2, pack_halo, 0)
 
-    pl.semaphore_wait(bar, SLICES + 3 + jnp.where(is_worker, 2 * BLOCKS - 2, 0))
+    pl.semaphore_wait(bar, SLICES + 1 - jnp.where(is_worker, 1, 0))
+    pl.semaphore_signal(ready, inc=1, device_id=(row, before), device_id_type=MESH)
 
     mine = pl.ds(pl.multiple_of(PAD + PITCH * blk, 8), PITCH)
 
@@ -182,18 +170,6 @@
 
     lax.fori_loop(0, SLICES, send_main, 0)
 
-    def const_copy():
-        return pltpu.make_async_remote_copy(
-            src_ref=cst.at[parity],
-            dst_ref=cst.at[parity],
-            send_sem=cst_s,
-            recv_sem=cst_r,
-            device_id=(row ^ 1, blk),
-            device_id_type=MESH,
-        )
-
-    const_copy().start()
-
     def wait_bytes(ref, sem):
         pltpu.make_async_copy(ref, ref, sem).wait()
 
@@ -215,10 +191,9 @@
             device_id_type=MESH,
         )
 
+    halo_copy(1).start()
+    pl.semaphore_wait(ready, 1)
     halo_copy(0).start()
-    halo_copy(1).start()
-    const_copy().wait_send()
-    wait_bytes(cst.at[1 - parity], cst_r)
 
     @pl.when(is_worker)
     def _():
@@ -237,20 +212,27 @@
             speed_axial + speed_pitch + speed_span
         ) * one(source == target)
         for rho in range(2):
-            both = still
-            for d in range(8):
-                both = both + jnp.where(
-                    source == (target + 16 * d) % 128, cst[rho, d : d + 1], 0.0
-                )
-            high, low = split(both)
             for half in range(2):
-                mix[rho, 128 * half : 128 * half + 128, 0:128] = high
                 mix[rho, 128 * half : 128 * half + 128, 128:256] = around.astype(jnp.bfloat16)
                 for q in range(3):
                     wide = one(source == 16 * (5 + q) + target % 16).astype(jnp.bfloat16)
                     mix[rho, 128 * half : 128 * half + 128, 256 + 128 * q : 384 + 128 * q] = wide
+        wait_bytes(many, main_r)
+        alive_to = []
+        for rho in range(2):
+            given = recv[rho, 2, PAD : PAD + 8]
+            table = jnp.zeros((8, 128), jnp.float32)
+            for v in range(NVAR):
+                column = jnp.broadcast_to(given[:, 112 + v : 113 + v], (8, 128))
+                table = jnp.where(slot8 == v, column, table)
+            alive_to.append(given[0:1, 112 + NVAR : 113 + NVAR])
+            both = still
+            for d in range(8):
+                both = both + jnp.where(source == (target + 16 * d) % 128, table[d : d + 1], 0.0)
+            high, low = split(both)
+            for half in range(2):
+                mix[rho, 128 * half : 128 * half + 128, 0:128] = high
             mix[rho, 256:384, 0:128] = low
-        wait_bytes(many, main_r)
         lane = lax.broadcasted_iota(jnp.int32, (CHUNK, 128), 1)
         slot = lane // 16
         cell = 8 * z - 4 + lane % 16
@@ -296,8 +278,7 @@
                 break
             factor = section_alphas[k] * time_step
             for rho in range(2):
-                table = cst[rho]
-                scale = jnp.where(cell_f < table[8:9], factor, 0.0)
+                scale = jnp.where(cell_f < alive_to[rho], factor, 0.0)
 
                 def update(i, c):
                     at = pl.multiple_of(i * CHUNK, CHUNK)
@@ -514,7 +495,6 @@
                 pltpu.SemaphoreType.DMA((4,)),
                 pltpu.VMEM((SLICES, 3, 8, 128), f32),
                 pltpu.VMEM((2, 3, NP + 2 * PAD, 128), f32),
-                pltpu.VMEM((2, 16, 128), f32),
                 pltpu.VMEM((2, NVAR + 1, AXIAL // 2, 8, 128), f32),
                 pltpu.VMEM((2, NVAR + 1, AXIAL // 2, 8, 128), f32),
                 pltpu.VMEM((2, 2, NP, 128), f32),
@@ -529,8 +509,7 @@
                 pltpu.VMEM((SECTIONS, NVAR, 16, 128), f32),
                 pltpu.SemaphoreType.DMA,
                 pltpu.SemaphoreType.DMA,
-                pltpu.SemaphoreType.DMA,
-                pltpu.SemaphoreType.DMA,
+                pltpu.SemaphoreType.REGULAR,
                 pltpu.SemaphoreType.DMA((2,)),
                 pltpu.SemaphoreType.DMA((2,)),
                 pltpu.SemaphoreType.DMA,

time: 75.1 us -> 74.5 us (level)
  no operation moved by 1% of the time
where the time goes in v4:
time: 74.5 us; the launch traced here: 74.2 us
  Pallas kernels  71.9 us (97%)
  local copies, waits for them, and re-layouts  1.72 us (2%)
    pallas_call x1, Pallas kernels, body(): pl.pallas_call(kernel, out_shape=jax.ShapeDtypeStruct((NVAR, AXIAL, PITCH...  71.9 us
    unnamed x1, local copies, waits for them, and re-layouts  1.72 us

profile of v4, /device:TPU:1, one launch (start us, length us, event | category | flops | bytes accessed | tf_op | source)
XLA Modules:
  0.0 74.2 jit_solution(6215548204701349396)
XLA Ops:
  0.7 71.9 %sections.1 = f32[5,16,8,128]{3,2,1,0:T(8,128)} custom-call(f32[5,16,8,128]{3,2,1,0:T(8,128)} %bitcast.5, f32[16,8,128]{2,1,0:T(8,128)} %bitcast.6, f32[5,1,5]{2,1,0:T(1,128)} %bitcast.7, s32[4,8]{1,0:T(4,128)} %offs.1, s32[1]{0:T(128)S(6)} %copy.9.live, bf16[32,512]{1,0:T(8,128)(2,1)} %constant.4.clone.basis_hbm, bf16[512,128]{1,0:T(8,128)(2,1)} %constant.5.clone.basis_t_hbm), custom_call_target="tpu_custom_call" | custom-call | tf_op jit(solution)/shard_map/sections/pallas_call | solution.py:483
  72.5 1.7 %copy.10 = f32[1,5,16,8,128]{4,3,2,1,0:T(8,128)} copy(f32[1,5,16,8,128]{4,3,2,1,0:T(8,128)} %bitcast.4) | data formatting | bytes 655360

commit v5 on v4

--- a/solution.py
+++ b/solution.py
@@ -55,7 +55,8 @@
 
 
 def worker_of(pair, s):
-    return 2 * pair + (s // 2) % 2, 4 * s + 2 * (s % 2) + 1
+    plane = 2 * (s // 2) + pair % 2
+    return 2 * pair + (s // 2) % 2, 4 * plane + 2 * (s % 2) + 1
 
 
 def kernel(
@@ -76,7 +77,8 @@
     blk = lax.axis_index("blk")
     pair, parity = row // 2, row % 2
     z = blk // 4
-    own_row, own_blk = worker_of(pair, z)
+    own = 2 * (z // 2) + (blk // 2) % 2
+    own_row, own_blk = worker_of(pair, own)
     is_worker = jnp.logical_and(own_row == row, own_blk == blk)
     after, before = (blk + 1) % BLOCKS, (blk + BLOCKS - 1) % BLOCKS
 
@@ -197,10 +199,10 @@
 
     @pl.when(is_worker)
     def _():
-        recv[parity, :, mine] = msg[z]
+        recv[parity, :, mine] = msg[own]
         source = lax.broadcasted_iota(jnp.int32, (128, 128), 0)
         target = lax.broadcasted_iota(jnp.int32, (128, 128), 1)
-        place = 8 * z - 4 + target % 16
+        place = 8 * own - 4 + target % 16
         lower = jnp.where(place == 0, target, target - 1)
         upper = jnp.where(place == SPAN - 1, target, target + 1)
 
@@ -235,7 +237,7 @@
             mix[rho, 256:384, 0:128] = low
         lane = lax.broadcasted_iota(jnp.int32, (CHUNK, 128), 1)
         slot = lane // 16
-        cell = 8 * z - 4 + lane % 16
+        cell = 8 * own - 4 + lane % 16
         cell_f = cell[0:1].astype(jnp.float32)
 
         def wrap(ref, *index):
@@ -363,7 +365,7 @@
                 def _():
                     pltpu.make_async_remote_copy(
                         src_ref=st.at[rho, :, source_rows],
-                        dst_ref=gbuf.at[z],
+                        dst_ref=gbuf.at[own],
                         send_sem=ret_s,
                         recv_sem=ret_r,
                         device_id=(other, at),
@@ -373,7 +375,7 @@
             return c
 
         lax.fori_loop(0, BLOCKS, send_back, 0)
-        gbuf[z] = st[parity, :, pl.ds(pl.multiple_of(PITCH * blk, 8), PITCH)]
+        gbuf[own] = st[parity, :, pl.ds(pl.multiple_of(PITCH * blk, 8), PITCH)]
 
     halo_copy(0).wait_recv()
     halo_copy(1).wait_recv()

time: 74.5 us -> 68.7 us (0.922)
  Pallas kernels: 71.9 us -> 66.1 us
    pallas_call x1, Pallas kernels: 71.9 us -> 66.1 us  [body(): pl.pallas_call(kernel, out_shape=jax.ShapeDtypeStruct((NVAR, AXIAL, PITCH...]
where the time goes in v5:
time: 68.7 us; the launch traced here: 68.5 us
  Pallas kernels  66.1 us (96%)
  local copies, waits for them, and re-layouts  1.72 us (3%)
    pallas_call x1, Pallas kernels, body(): pl.pallas_call(kernel, out_shape=jax.ShapeDtypeStruct((NVAR, AXIAL, PITCH...  66.1 us
    unnamed x1, local copies, waits for them, and re-layouts  1.72 us

profile of v5, /device:TPU:1, one launch (start us, length us, event | category | flops | bytes accessed | tf_op | source)
XLA Modules:
  0.0 68.5 jit_solution(4357998074122569075)
XLA Ops:
  0.7 66.1 %sections.1 = f32[5,16,8,128]{3,2,1,0:T(8,128)} custom-call(f32[5,16,8,128]{3,2,1,0:T(8,128)} %bitcast.5, f32[16,8,128]{2,1,0:T(8,128)} %bitcast.6, f32[5,1,5]{2,1,0:T(1,128)} %bitcast.7, s32[4,8]{1,0:T(4,128)} %offs.1, s32[1]{0:T(128)S(6)} %copy.9.live, bf16[32,512]{1,0:T(8,128)(2,1)} %constant.4.clone.basis_hbm, bf16[512,128]{1,0:T(8,128)(2,1)} %constant.5.clone.basis_t_hbm), custom_call_target="tpu_custom_call" | custom-call | tf_op jit(solution)/shard_map/sections/pallas_call | solution.py:485
  66.8 1.7 %copy.10 = f32[1,5,16,8,128]{4,3,2,1,0:T(8,128)} copy(f32[1,5,16,8,128]{4,3,2,1,0:T(8,128)} %bitcast.4) | data formatting | bytes 655360

commit v6 on v5

--- a/solution.py
+++ b/solution.py
@@ -60,19 +60,11 @@
 
 
 def kernel(
-    state_hbm, visc_hbm, coup, offs, live, basis_hbm, basis_t_hbm, out,
-    state, visc, basis, basis_t, mix, size, load_s,
+    state_hbm, visc_hbm, coup_hbm, offs_hbm, live_hbm, basis_hbm, basis_t_hbm, out,
+    state, visc, basis, basis_t, mix, size, coup, offs, live, load_s,
     msg, recv, hs, hr, vb, xa, xb, xc, hb, st, gbuf, fld, vext, gx,
     main_s, main_r, ready, halo_s, halo_r, ret_s, ret_r,
 ):
-    loads = [
-        pltpu.make_async_copy(source, target, load_s.at[i])
-        for i, (source, target) in enumerate(
-            [(state_hbm, state), (visc_hbm, visc), (basis_hbm, basis), (basis_t_hbm, basis_t)]
-        )
-    ]
-    for load in loads:
-        load.start()
     row = lax.axis_index("row")
     blk = lax.axis_index("blk")
     pair, parity = row // 2, row % 2
@@ -104,6 +96,18 @@
         lax.fori_loop(0, BLOCKS, greet_source, 0)
 
     greet(row, after)
+
+    loads = [
+        pltpu.make_async_copy(source, target, load_s.at[i])
+        for i, (source, target) in enumerate(
+            [
+                (state_hbm, state), (visc_hbm, visc), (basis_hbm, basis), (basis_t_hbm, basis_t),
+                (coup_hbm, coup), (offs_hbm, offs), (live_hbm, live),
+            ]
+        )
+    ]
+    for load in loads:
+        load.start()
 
     for load in loads:
         load.wait()
@@ -346,36 +350,34 @@
                 both = jnp.where(inside, part[0], pltpu.roll(part[1], 8, 1))
                 third = jnp.where(inside, pltpu.roll(part[2], 80, 1), pltpu.roll(part[2], 40, 1))
                 both = jnp.where(lane < 84, both, third)
-                st[rho, 0, pl.ds(at, CHUNK)] = both
-                st[rho, 1, pl.ds(at, CHUNK - 8)] = both[8:CHUNK]
-                before_at = pl.multiple_of((at + NP - 8) % NP, 8)
-                st[rho, 1, pl.ds(before_at, 8)] = both[0:8]
-                st[rho, 2, pl.ds(at, CHUNK)] = part[3]
+                blocks = both.reshape(BLOCKS, PITCH, 128)
+                st[rho, :, 0] = blocks
+                st[rho, 0 : BLOCKS - 1, 1] = blocks[1:]
+                st[rho, BLOCKS - 1, 1] = blocks[0]
+                st[rho, :, 2] = part[3].reshape(BLOCKS, PITCH, 128)
                 return c
 
             lax.fori_loop(0, NP // CHUNK, pack_back, 0)
 
-        def send_back(i, c):
+        def send_back(other, at):
+            pltpu.make_async_remote_copy(
+                src_ref=st.at[other % 2, at],
+                dst_ref=gbuf.at[own],
+                send_sem=ret_s,
+                recv_sem=ret_r,
+                device_id=(other, at),
+                device_id_type=MESH,
+            ).start()
+
+        def send_both(i, c):
             at = (blk + BLOCKS // 2 + jnp.where(i % 2 == 1, (i + 1) // 2, BLOCKS - i // 2)) % BLOCKS
-            source_rows = pl.ds(pl.multiple_of(PITCH * at, 8), PITCH)
-            for rho in range(2):
-                other = 2 * pair + rho
-
-                @pl.when(jnp.logical_not(jnp.logical_and(other == row, at == blk)))
-                def _():
-                    pltpu.make_async_remote_copy(
-                        src_ref=st.at[rho, :, source_rows],
-                        dst_ref=gbuf.at[own],
-                        send_sem=ret_s,
-                        recv_sem=ret_r,
-                        device_id=(other, at),
-                        device_id_type=MESH,
-                    ).start()
-
+            send_back(row ^ 1, at)
+            send_back(row, at)
             return c
 
-        lax.fori_loop(0, BLOCKS, send_back, 0)
-        gbuf[own] = st[parity, :, pl.ds(pl.multiple_of(PITCH * blk, 8), PITCH)]
+        lax.fori_loop(0, BLOCKS - 1, send_both, 0, unroll=3)
+        send_back(row ^ 1, blk)
+        gbuf[own] = st[parity, blk]
 
     halo_copy(0).wait_recv()
     halo_copy(1).wait_recv()
@@ -480,12 +482,11 @@
     def body(state, visc, coup, offs, live):
         vmem = pl.BlockSpec(memory_space=pltpu.VMEM)
         hbm = pl.BlockSpec(memory_space=pltpu.HBM)
-        smem = pl.BlockSpec(memory_space=pltpu.SMEM)
         f32 = jnp.float32
         done = pl.pallas_call(
             kernel,
             out_shape=jax.ShapeDtypeStruct((NVAR, AXIAL, PITCH, SPAN), f32),
-            in_specs=[hbm, hbm, smem, smem, smem, hbm, hbm],
+            in_specs=[hbm] * 7,
             out_specs=vmem,
             scratch_shapes=[
                 pltpu.VMEM((NVAR, AXIAL, PITCH, SPAN), f32),
@@ -494,7 +495,10 @@
                 pltpu.VMEM((NP, 128), jnp.bfloat16),
                 pltpu.VMEM((2, 384, 640), jnp.bfloat16),
                 pltpu.VMEM((2 * BLOCKS, 3, 8, 128), f32),
-                pltpu.SemaphoreType.DMA((4,)),
+                pltpu.SMEM((NVAR, 1, NVAR), f32),
+                pltpu.SMEM((4, 8), jnp.int32),
+                pltpu.SMEM((1,), jnp.int32),
+                pltpu.SemaphoreType.DMA((7,)),
                 pltpu.VMEM((SLICES, 3, 8, 128), f32),
                 pltpu.VMEM((2, 3, NP + 2 * PAD, 128), f32),
                 pltpu.VMEM((2, NVAR + 1, AXIAL // 2, 8, 128), f32),
@@ -504,7 +508,7 @@
                 pltpu.VMEM((2, 2, NP + 2 * PAD, 128), f32),
                 pltpu.VMEM((2, NP + 2 * PAD, 128), f32),
                 pltpu.VMEM((SECTIONS, 2, NP + WRAP, 128), f32),
-                pltpu.VMEM((2, 3, NP, 128), f32),
+                pltpu.VMEM((2, BLOCKS, 3, 8, 128), f32),
                 pltpu.VMEM((SLICES, 3, 8, 128), f32),
                 pltpu.VMEM((SECTIONS, NVAR, AXIAL, 16, 128), f32),
                 pltpu.VMEM((AXIAL, 16, 128), f32),

time: 68.7 us -> 68 us (0.990)
  Pallas kernels: 66.1 us -> 65.4 us
where the time goes in v6:
time: 68 us; the launch traced here: 67.8 us
  Pallas kernels  65.4 us (96%)
  local copies, waits for them, and re-layouts  1.72 us (3%)
    pallas_call x1, Pallas kernels, body(): pl.pallas_call(kernel, out_shape=jax.ShapeDtypeStruct((NVAR, AXIAL, PITCH...  65.4 us
    unnamed x1, local copies, waits for them, and re-layouts  1.72 us

profile of v6, /device:TPU:1, one launch (start us, length us, event | category | flops | bytes accessed | tf_op | source)
XLA Modules:
  0.0 67.8 jit_solution(6319620324247775537)
XLA Ops:
  0.7 65.4 %sections.1 = f32[5,16,8,128]{3,2,1,0:T(8,128)} custom-call(f32[5,16,8,128]{3,2,1,0:T(8,128)} %bitcast.5, f32[16,8,128]{2,1,0:T(8,128)} %bitcast.6, f32[5,1,5]{2,1,0:T(1,128)} %bitcast.7, s32[4,8]{1,0:T(4,128)} %offs_hbm.1, s32[1]{0:T(128)S(6)} %copy.9.live_hbm, bf16[32,512]{1,0:T(8,128)(2,1)} %constant.4.clone.basis_hbm, ...), custom_call_target="tpu_custom_call" | custom-call | tf_op jit(solution)/shard_map/sections/pallas_call | solution.py:486
  66.1 1.7 %copy.10 = f32[1,5,16,8,128]{4,3,2,1,0:T(8,128)} copy(f32[1,5,16,8,128]{4,3,2,1,0:T(8,128)} %bitcast.4) | data formatting | bytes 655360

commit v7 on v6

--- a/solution.py
+++ b/solution.py
@@ -370,13 +370,12 @@
             ).start()
 
         def send_both(i, c):
-            at = (blk + BLOCKS // 2 + jnp.where(i % 2 == 1, (i + 1) // 2, BLOCKS - i // 2)) % BLOCKS
-            send_back(row ^ 1, at)
-            send_back(row, at)
+            send_back(row ^ 1, i)
+            send_back(row, i + jnp.where(i >= blk, 1, 0))
             return c
 
         lax.fori_loop(0, BLOCKS - 1, send_both, 0, unroll=3)
-        send_back(row ^ 1, blk)
+        send_back(row ^ 1, BLOCKS - 1)
         gbuf[own] = st[parity, blk]
 
     halo_copy(0).wait_recv()

time: 68 us -> 63.4 us (0.932)
  Pallas kernels: 65.4 us -> 60.8 us
    pallas_call x1, Pallas kernels: 65.4 us -> 60.8 us  [body(): pl.pallas_call(kernel, out_shape=jax.ShapeDtypeStruct((NVAR, AXIAL, PITCH...]
where the time goes in v7:
time: 63.4 us; the launch traced here: 63.1 us
  Pallas kernels  60.8 us (96%)
  local copies, waits for them, and re-layouts  1.72 us (3%)
  between operations  0.66 us (1%)
    pallas_call x1, Pallas kernels, body(): pl.pallas_call(kernel, out_shape=jax.ShapeDtypeStruct((NVAR, AXIAL, PITCH...  60.8 us
    unnamed x1, local copies, waits for them, and re-layouts  1.72 us

profile of v7, /device:TPU:1, one launch (start us, length us, event | category | flops | bytes accessed | tf_op | source)
XLA Modules:
  0.0 63.1 jit_solution(10367709317978363360)
XLA Ops:
  0.7 60.8 %sections.1 = f32[5,16,8,128]{3,2,1,0:T(8,128)} custom-call(f32[5,16,8,128]{3,2,1,0:T(8,128)} %bitcast.5, f32[16,8,128]{2,1,0:T(8,128)} %bitcast.6, f32[5,1,5]{2,1,0:T(1,128)} %bitcast.7, s32[4,8]{1,0:T(4,128)} %offs_hbm.1, s32[1]{0:T(128)S(6)} %copy.9.live_hbm, bf16[32,512]{1,0:T(8,128)(2,1)} %constant.4.clone.basis_hbm, ...), custom_call_target="tpu_custom_call" | custom-call | tf_op jit(solution)/shard_map/sections/pallas_call | solution.py:485
  61.4 1.7 %copy.10 = f32[1,5,16,8,128]{4,3,2,1,0:T(8,128)} copy(f32[1,5,16,8,128]{4,3,2,1,0:T(8,128)} %bitcast.4) | data formatting | bytes 655360

commit v8 on v7

--- a/solution.py
+++ b/solution.py
@@ -55,8 +55,8 @@
 
 
 def worker_of(pair, s):
-    plane = 2 * (s // 2) + pair % 2
-    return 2 * pair + (s // 2) % 2, 4 * plane + 2 * (s % 2) + 1
+    plane = s // 2
+    return 2 * pair + (plane + pair) % 2, 4 * plane + 2 * (s % 2) + 1
 
 
 def kernel(
@@ -69,7 +69,7 @@
     blk = lax.axis_index("blk")
     pair, parity = row // 2, row % 2
     z = blk // 4
-    own = 2 * (z // 2) + (blk // 2) % 2
+    own = 2 * (z % (SLICES // 2)) + (blk // 2) % 2
     own_row, own_blk = worker_of(pair, own)
     is_worker = jnp.logical_and(own_row == row, own_blk == blk)
     after, before = (blk + 1) % BLOCKS, (blk + BLOCKS - 1) % BLOCKS
@@ -157,7 +157,7 @@
     mine = pl.ds(pl.multiple_of(PAD + PITCH * blk, 8), PITCH)
 
     def send_main(i, c):
-        s = (z + SLICES // 2 + jnp.where(i % 2 == 1, (i + 1) // 2, SLICES - i // 2)) % SLICES
+        s = (2 * z + SLICES // 2 + jnp.where(i % 2 == 1, (i + 1) // 2, SLICES - i // 2)) % SLICES
         wr, wb = worker_of(pair, s)
         self = jnp.logical_and(wr == row, wb == blk)
 

time: 63.4 us -> 70.1 us (1.11)
  the two profiles are of different devices: /device:TPU:1 before, /device:TPU:899 now
where the time goes in v8:
time: 70.1 us; the launch traced here: 69.9 us
  Pallas kernels  67.5 us (96%)
  local copies, waits for them, and re-layouts  1.72 us (2%)
    pallas_call x1, Pallas kernels, body(): pl.pallas_call(kernel, out_shape=jax.ShapeDtypeStruct((NVAR, AXIAL, PITCH...  67.5 us
    unnamed x1, local copies, waits for them, and re-layouts  1.72 us

profile of v8, /device:TPU:899, one launch (start us, length us, event | category | flops | bytes accessed | tf_op | source)
XLA Modules:
  0.0 69.9 jit_solution(5946148290425852935)
XLA Ops:
  0.7 67.5 %sections.1 = f32[5,16,8,128]{3,2,1,0:T(8,128)} custom-call(f32[5,16,8,128]{3,2,1,0:T(8,128)} %bitcast.5, f32[16,8,128]{2,1,0:T(8,128)} %bitcast.6, f32[5,1,5]{2,1,0:T(1,128)} %bitcast.7, s32[4,8]{1,0:T(4,128)} %offs_hbm.1, s32[1]{0:T(128)S(6)} %copy.9.live_hbm, bf16[32,512]{1,0:T(8,128)(2,1)} %constant.4.clone.basis_hbm, ...), custom_call_target="tpu_custom_call" | custom-call | tf_op jit(solution)/shard_map/sections/pallas_call | solution.py:485
  68.2 1.7 %copy.10 = f32[1,5,16,8,128]{4,3,2,1,0:T(8,128)} copy(f32[1,5,16,8,128]{4,3,2,1,0:T(8,128)} %bitcast.4) | data formatting | bytes 655360

commit v9 on v7

--- a/solution.py
+++ b/solution.py
@@ -433,7 +433,7 @@
             layer(k, a, lambda v: fld[k, v, a + 1])
             return c
 
-        lax.fori_loop(0, AXIAL - 1 - k, inner_layer, 0)
+        lax.fori_loop(0, AXIAL - 1 - k, inner_layer, 0, unroll=True)
 
     @pl.when(is_worker)
     def _():

time: 63.4 us -> 63.3 us (level)
  no operation moved by 1% of the time
where the time goes in v9:
time: 63.3 us; the launch traced here: 63.2 us
  Pallas kernels  60.8 us (96%)
  local copies, waits for them, and re-layouts  1.72 us (3%)
  between operations  0.66 us (1%)
    pallas_call x1, Pallas kernels, body(): pl.pallas_call(kernel, out_shape=jax.ShapeDtypeStruct((NVAR, AXIAL, PITCH...  60.8 us
    unnamed x1, local copies, waits for them, and re-layouts  1.72 us

profile of v9, /device:TPU:1, one launch (start us, length us, event | category | flops | bytes accessed | tf_op | source)
XLA Modules:
  0.0 63.2 jit_solution(13784256431671613673)
XLA Ops:
  0.7 60.8 %sections.1 = f32[5,16,8,128]{3,2,1,0:T(8,128)} custom-call(f32[5,16,8,128]{3,2,1,0:T(8,128)} %bitcast.5, f32[16,8,128]{2,1,0:T(8,128)} %bitcast.6, f32[5,1,5]{2,1,0:T(1,128)} %bitcast.7, s32[4,8]{1,0:T(4,128)} %offs_hbm.1, s32[1]{0:T(128)S(6)} %copy.9.live_hbm, bf16[32,512]{1,0:T(8,128)(2,1)} %constant.4.clone.basis_hbm, ...), custom_call_target="tpu_custom_call" | custom-call | tf_op jit(solution)/shard_map/sections/pallas_call | solution.py:485
  61.4 1.7 %copy.10 = f32[1,5,16,8,128]{4,3,2,1,0:T(8,128)} copy(f32[1,5,16,8,128]{4,3,2,1,0:T(8,128)} %bitcast.4) | data formatting | bytes 655360
